TPU v7x, 32 devices: a whole 2x2x4 slice. The times are simulated.
32 devices in a mesh: occ: 16 (over z, y, x), vir: 2 (over core).
Axes of the slice: x: 2, y: 2, z: 4, core: 2. Of those that a mesh axis runs over, the one named last changes fastest.
Arguments:
- amplitudes: bfloat16 [64, 8, 64, 4096], P(('occ', 'vir')), may hold values from -6 to 6
- tile_counts: int32 [64], P(('occ', 'vir')), may hold values from 1 to 8, 384 in all
- tile_owner: int32 [64, 8], P(('occ', 'vir')), may hold values from 0 to 15, all different within a row; in each aligned block of 2 rows (0 to 1, 2 to 3, ...) at most 2 rows name the same one
- tile_local: int32 [64, 8], P(('occ', 'vir')), may hold values from 0 to 15
- pair_map: int32 [256], replicated, may hold values from 0 to 255, each once
- hole_weight: bfloat16 [64, 64, 64], P(('occ', 'vir')), may hold values from -0.75 to 0.75
- fock_tiles: bfloat16 [16, 64, 64], replicated, may hold values from -0.75 to 0.75
- ladder_panels: bfloat16 [256, 4096, 128], P('occ', 'vir'), may hold values from -0.03125 to 0.03125
Outputs:
- local_residual: bfloat16 [64, 8, 64, 4096], P(('occ', 'vir'))
- ladder_panel: bfloat16 [64, 64, 128], P(('occ', 'vir'))
Inputs may be any that keep to these rules, and one draw needn't show every extreme that they name: `tile_counts`: entries of a list at or past its count are not used. `tile_owner`: the 8 entries of a pair tile name different owners; among the pair tiles of one device no owner is named by more than 2 entries. `pair_map`: every virtual tile pair stands at exactly one owner position.
All inputs are finite; a program needn't handle non-finite values. No bound on the sum of `tile_counts` on one device may be relied on, other than what follows from the above.
Results may differ from a plain program's by a relative error of at most 0.001.
Values may be sent and summed in bfloat16 or wider, within the bound.
No kernel may reach another device: no remote copies, remote signals or barrier semaphores. Data moves between devices by JAX's collectives and lax.ppermute only.
A program may use at most 320 MiB of HBM per device.

v0:
```python
import jax
import jax.numpy as jnp
from jax import lax
from jax.sharding import PartitionSpec as P

CAP = 2


def per_device(
    amplitudes,
    tile_counts,
    tile_owner,
    tile_local,
    pair_map,
    hole_weight,
    fock_tiles,
    ladder_panels,
):
    owners = lax.axis_size("occ")
    per_owner = ladder_panels.shape[0]
    panel_width = ladder_panels.shape[2]
    tile_count = fock_tiles.shape[0]
    tile_width = fock_tiles.shape[1]
    local_tiles, slot_count, pair_rows, tile_size = amplitudes.shape
    whole_tiles = pair_map.shape[0]
    used_slot = jnp.arange(slot_count, dtype=jnp.int32)[None, :] < tile_counts[:, None]
    tile_pos = tile_owner * per_owner + tile_local
    flat_owner = tile_owner.reshape(-1)
    owner_hits = (flat_owner[:, None] == jnp.arange(owners, dtype=jnp.int32)[None, :]).astype(
        jnp.int32
    )
    earlier = jnp.cumsum(owner_hits, axis=0) - owner_hits
    slot_rank = jnp.sum(earlier * owner_hits, axis=1)
    send_index = flat_owner * CAP + slot_rank
    kept = jnp.where(used_slot[:, :, None, None], amplitudes, jnp.zeros((), jnp.bfloat16))
    kept = kept.reshape(local_tiles * slot_count, pair_rows, tile_size)
    outgoing = (
        jnp.zeros((owners * CAP, pair_rows, tile_size), jnp.bfloat16).at[send_index].set(kept)
    )
    outgoing = outgoing.reshape(owners, CAP, pair_rows, tile_size)
    marked = jnp.where(used_slot, tile_local, -1).reshape(-1)
    out_slot = (
        jnp.full((owners * CAP,), -1, jnp.int32).at[send_index].set(marked).reshape(owners, CAP)
    )
    arrived, arrived_slot = (
        lax.all_to_all(outgoing, "occ", split_axis=0, concat_axis=0, tiled=True),
        lax.all_to_all(out_slot, "occ", split_axis=0, concat_axis=0, tiled=True),
    )
    selector = (
        arrived_slot[:, :, None] == jnp.arange(per_owner, dtype=jnp.int32)[None, None, :]
    ).astype(jnp.bfloat16)
    chosen = jnp.einsum(
        "ock,knq->ocnq",
        selector,
        lax.all_gather(ladder_panels, "vir", axis=1, tiled=True),
        preferred_element_type=jnp.float32,
    ).astype(jnp.bfloat16)
    partial_value = jnp.einsum(
        "ocpn,ocnq->ocpq", arrived, chosen, preferred_element_type=jnp.float32
    )
    returned = lax.all_to_all(partial_value, "occ", split_axis=0, concat_axis=0, tiled=True)
    match_pos = tile_pos[:, :, None] == jnp.arange(whole_tiles, dtype=jnp.int32)[None, None, :]
    tile_ident = jnp.sum(jnp.where(match_pos, pair_map[None, None, :], 0), axis=2)
    tile_range = jnp.arange(tile_count, dtype=jnp.int32)[None, None, :]
    pick_rows = ((tile_ident // tile_count)[:, :, None] == tile_range).astype(jnp.bfloat16)
    pick_cols = ((tile_ident % tile_count)[:, :, None] == tile_range).astype(jnp.bfloat16)
    left_fock = jnp.einsum(
        "Psn,nce->Psce", pick_rows, fock_tiles, preferred_element_type=jnp.float32
    ).astype(jnp.bfloat16)
    right_fock = jnp.einsum(
        "Psn,nce->Psce", pick_cols, fock_tiles, preferred_element_type=jnp.float32
    ).astype(jnp.bfloat16)
    hole = jnp.einsum("Ppq,Psqx->Pspx", hole_weight, amplitudes, preferred_element_type=jnp.float32)
    shaped = amplitudes.reshape(local_tiles, slot_count, pair_rows, tile_width, tile_width)
    fock_part = jnp.einsum(
        "Pspce,Psed->Pspcd", shaped, right_fock, preferred_element_type=jnp.float32
    )
    fock_part = fock_part + jnp.einsum(
        "Psce,Psped->Pspcd", left_fock, shaped, preferred_element_type=jnp.float32
    )
    summed = hole + fock_part.reshape(local_tiles, slot_count, pair_rows, tile_size)
    local_residual = jnp.where(used_slot[:, :, None, None], summed, 0.0).astype(jnp.bfloat16)
    flat_back = returned.reshape(owners * CAP, pair_rows, panel_width)
    per_slot = flat_back[send_index].reshape(local_tiles, slot_count, pair_rows, panel_width)
    ladder_panel = jnp.sum(jnp.where(used_slot[:, :, None, None], per_slot, 0.0), axis=1).astype(
        jnp.bfloat16
    )
    return (local_residual, ladder_panel)


def solution(mesh):
    in_specs = (
        P(("occ", "vir"), None, None, None),
        P(("occ", "vir")),
        P(("occ", "vir"), None),
        P(("occ", "vir"), None),
        P(),
        P(("occ", "vir"), None, None),
        P(),
        P("occ", "vir", None),
    )
    out_specs = (P(("occ", "vir"), None, None, None), P(("occ", "vir"), None, None))
    return jax.shard_map(
        per_device, mesh=mesh, in_specs=in_specs, out_specs=out_specs, check_vma=False
    )
```

profile of v0, /device:TPU:0, one launch (start us, length us, event | category | flops | bytes accessed | tf_op | source)
XLA Modules:
  0.0 590.2 jit_solution(2127145730472181451)
XLA Ops:
  7.2 0.8 eq.80
  7.9 0.8 broadcast_select_fusion.1
  9.2 0.6 scatter_custom_fusion.1
  9.8 0.7 all_to_all.13
  10.5 8.3 %all-to-all-start.1 = ((s32[16,1,2]{2,1,0:T(1,128)}), s32[16,1,2]{2,1,0:T(1,128)S(1)}, u32[]{:S(2)}, u32[]{:S(2)}) async-start(s32[16,1,2]{2,1,0:T(1,128)} %bitcast.17), calls=%async_computation.1 | async-start | bytes 16384 | tf_op jit(solution)/shard_map/all_to_all | solution.py:47
  18.8 0.7 iota_compare_fusion.5
  19.6 7.4 %broadcast_select_fusion = bf16[2,8,64,4096]{3,2,1,0:T(8,128)(2,1)} fusion(bf16[2,8,64,4096]{3,2,1,0:T(8,128)(2,1)} %param.8, pred[2,8]{1,0:T(4,128)(4,1)S(1)} %iota_compare_fusion.5), kind=kLoop, calls=%fused_computation.11 | loop fusion | flops 4194304 | bytes 16777232 | tf_op jit(solution)/shard_map/jit(_where)/select_n | solution.py:35
  26.9 5.9 %broadcast_in_dim.76 = bf16[32,64,4096]{2,1,0:T(8,128)(2,1)} broadcast(bf16[]{:T(256)} %constant.43.clone.1), dimensions={} | broadcast | bytes 16777218 | tf_op jit(solution)/shard_map/broadcast_in_dim | solution.py:38
  32.9 21.3 %scatter_fusion = bf16[32,64,4096]{2,1,0:T(8,128)(2,1)} fusion(bf16[32,64,4096]{2,1,0:T(8,128)(2,1)} %broadcast_in_dim.76, s32[16]{0:T(128)S(1)} %fusion.25, bf16[16,64,4096]{2,1,0:T(8,128)(2,1)} %bitcast.65), kind=kCustom, calls=%fused_computation.1 | custom fusion | bytes 25165888 | tf_op jit(solution)/shard_map/scatter | solution.py:38
  54.2 6.9 %all-to-all-start = ((bf16[16,2,64,4096]{3,2,1,0:T(8,128)(2,1)}), bf16[16,2,64,4096]{3,2,1,0:T(8,128)(2,1)}, u32[]{:S(2)}, u32[]{:S(2)}) async-start(bf16[16,2,64,4096]{3,2,1,0:T(8,128)(2,1)} %bitcast.64), calls=%async_computation | async-start | bytes 33554432 | tf_op jit(solution)/shard_map/all_to_all | solution.py:46
  61.2 10.3 %copy.46 = bf16[16,2048,128]{2,0,1:T(8,128)(2,1)} copy(bf16[16,2048,128]{2,1,0:T(8,128)(2,1)} %param.15) | data formatting | bytes 16777216 | tf_op args[7]
  71.5 24.1 %reshape.114 = bf16[2,8,64,64,64]{4,3,2,1,0:T(8,128)(2,1)} reshape(bf16[2,8,64,4096]{3,2,1,0:T(8,128)(2,1)} %param.8) | data formatting | bytes 16777216 | tf_op jit(solution)/shard_map/reshape | solution.py:74
  95.9 0.3 fusion.5
  96.4 24.1 %fusion.8 = f32[2,8,64,64,64]{4,2,3,1,0:T(8,128)} fusion(bf16[2,8,64,64,64]{4,3,2,1,0:T(8,128)(2,1)} %reshape.114, bf16[2,8,64,64,1]{3,1,2,0,4:T(8,128)(2,1)S(1)} %fusion.5), kind=kOutput, calls=%fused_computation.18 | convolution fusion | flops 536870912 | bytes 25296896 | tf_op jit(solution)/shard_map/Pspce,Psed->Pspcd/dot_general | solution.py:75
  120.6 23.1 %convolution_convert_fusion = bf16[16,2,4096,128]{3,0,2,1:T(8,128)(2,1)} fusion(bf16[16,4096,128]{2,0,1:T(8,128)(2,1)} %all-gather.2.cloned.1.call-done, s32[16,2]{0,1:T(2,128)S(1)} %bitcast.67), kind=kOutput, calls=%fused_computation.6 | convolution fusion | flops 553648640 | bytes 50331776 | tf_op jit(solution)/shard_map/ock,knq->ocnq/dot_general | solution.py:52
  143.7 232.1 %all-to-all-done = bf16[16,2,64,4096]{3,2,1,0:T(8,128)(2,1)} async-done(((bf16[16,2,64,4096]{3,2,1,0:T(8,128)(2,1)}), bf16[16,2,64,4096]{3,2,1,0:T(8,128)(2,1)}, u32[]{:S(2)}, u32[]{:S(2)}) %all-to-all-start) | async-done | bytes 16777248 | tf_op jit(solution)/shard_map/all_to_all | solution.py:46
  375.8 32.5 %fusion = f32[16,2,64,128]{3,2,1,0:T(8,128)} fusion(bf16[16,2,64,4096]{3,2,1,0:T(8,128)(2,1)} %all-to-all-done, bf16[16,2,4096,128]{3,0,2,1:T(8,128)(2,1)} %convolution_convert_fusion), kind=kOutput, calls=%fused_computation.4 | convolution fusion | flops 2147483648 | bytes 51380224 | tf_op jit(solution)/shard_map/ocpn,ocnq->ocpq/dot_general | solution.py:58
  408.3 72.1 %all-to-all-start.2 = ((f32[16,2,64,128]{3,2,1,0:T(8,128)}), f32[16,2,64,128]{3,2,1,0:T(8,128)S(1)}, u32[]{:S(2)}, u32[]{:S(2)}) async-start(f32[16,2,64,128]{3,2,1,0:T(8,128)} %fusion), calls=%async_computation.2 | async-start | bytes 2097152 | tf_op jit(solution)/shard_map/all_to_all | solution.py:61
  480.4 28.8 %bitcast_add_fusion = f32[2,8,64,64,64]{3,4,2,1,0:T(8,128)} fusion(f32[2,8,64,64,64]{4,2,3,1,0:T(8,128)} %fusion.8, bf16[2,8,64,64,64]{4,3,2,1,0:T(8,128)(2,1)} %reshape.114, bf16[2,8,64,64,1]{3,1,2,0,4:T(8,128)(2,1)S(1)} %fusion.6), kind=kOutput, calls=%fused_computation.3 | convolution fusion | flops 541065216 | bytes 42074112 | tf_op jit(solution)/shard_map/Psce,Psped->Pspcd/dot_general | solution.py:78
  509.2 31.1 %copy.43 = f32[2,8,64,64,64]{4,3,2,1,0:T(8,128)} copy(f32[2,8,64,64,64]{3,4,2,1,0:T(8,128)} %bitcast_add_fusion) | data formatting | bytes 33554432 | tf_op jit(solution)/shard_map/add | solution.py:78
  540.3 27.9 %reshape.115 = f32[2,8,64,4096]{3,2,1,0:T(8,128)} reshape(f32[2,8,64,64,64]{4,3,2,1,0:T(8,128)} %copy.43) | data formatting | bytes 33554432 | tf_op jit(solution)/shard_map/reshape | solution.py:81
  568.2 13.9 %fusion.4 = bf16[2,8,64,4096]{3,2,1,0:T(8,128)(2,1)} fusion(f32[2,8,64,4096]{3,2,1,0:T(8,128)} %reshape.115, bf16[2,8,64,4096]{3,2,1,0:T(8,128)(2,1)} %param.8, pred[2,8]{1,0:T(4,128)(4,1)S(1)} %iota_compare_fusion.5, bf16[2,64,64]{2,1,0:T(8,128)(2,1)S(1)} %copy-done), kind=kOutput, calls=%fused_computation.10 | convolution fusion | flops 549453824 | bytes 33570832 | tf_op jit(solution)/shard_map/Ppq,Psqx->Pspx/dot_general | solution.py:73
  582.1 0.6 gather_fusion
  582.7 0.7 select_reduce_fusion
  (22 shorter events, 1.1 us)
Async XLA Ops:
  7.2 561.0 %copy-start = (bf16[2,64,64]{2,1,0:T(8,128)(2,1)S(1)}, bf16[2,64,64]{2,1,0:T(8,128)(2,1)}, u32[]{:S(2)}) copy-start(bf16[2,64,64]{2,1,0:T(8,128)(2,1)} %param.13) | copy-start | bytes 49156
  10.5 43.6 %all-to-all-start.1 = ((s32[16,1,2]{2,1,0:T(1,128)}), s32[16,1,2]{2,1,0:T(1,128)S(1)}, u32[]{:S(2)}, u32[]{:S(2)}) async-start(s32[16,1,2]{2,1,0:T(1,128)} %bitcast.17), calls=%async_computation.1 | async-start | bytes 16384 | tf_op jit(solution)/shard_map/all_to_all | solution.py:47
  54.2 321.6 %all-to-all-start = ((bf16[16,2,64,4096]{3,2,1,0:T(8,128)(2,1)}), bf16[16,2,64,4096]{3,2,1,0:T(8,128)(2,1)}, u32[]{:S(2)}, u32[]{:S(2)}) async-start(bf16[16,2,64,4096]{3,2,1,0:T(8,128)(2,1)} %bitcast.64), calls=%async_computation | async-start | bytes 33554432 | tf_op jit(solution)/shard_map/all_to_all | solution.py:46
  61.1 59.5 %all-gather.2.cloned.1.call-start = ((), (), s32[]{:S(2)}) async-start(), calls=%async_computation.3 | async-start | bytes 25165824 | tf_op jit(solution)/shard_map/all_gather | solution.py:55
  71.5 24.1 %copy-start.2 = (s32[256]{0:T(256)S(1)}, s32[256]{0:T(256)}, u32[]{:S(2)}) copy-start(s32[256]{0:T(256)} %param.12) | copy-start | bytes 3076
  71.5 24.4 %copy-start.1 = (bf16[16,64,64]{2,1,0:T(8,128)(2,1)S(1)}, bf16[16,64,64]{2,1,0:T(8,128)(2,1)}, u32[]{:S(2)}) copy-start(bf16[16,64,64]{2,1,0:T(8,128)(2,1)} %param.14) | copy-start | bytes 393220
  408.3 173.8 %all-to-all-start.2 = ((f32[16,2,64,128]{3,2,1,0:T(8,128)}), f32[16,2,64,128]{3,2,1,0:T(8,128)S(1)}, u32[]{:S(2)}, u32[]{:S(2)}) async-start(f32[16,2,64,128]{3,2,1,0:T(8,128)} %fusion), calls=%async_computation.2 | async-start | bytes 2097152 | tf_op jit(solution)/shard_map/all_to_all | solution.py:61
Sparse Core Ops, SparseCore 0:
  71.6 31.3 all-gather.1
where the time goes:
time: 592 us; the launch traced here: 590 us
  waiting for transfers between devices  232 us (39%)
  local copies, waits for them, and re-layouts  124 us (21%)
  matrix products  123 us (21%)
  starting transfers between devices  87.4 us (15%)
  between operations  14.1 us (2%)
  other arithmetic  10.1 us (2%)
    all_to_all x1, waiting for transfers between devices, per_device(): lax.all_to_all(outgoing, 'occ', split_axis=0, concat_axis=0, tiled=True)  232 us
    all_to_all x1, starting transfers between devices, per_device(): lax.all_to_all(partial_value, 'occ', split_axis=0, concat_axis=0, tiled=T...  72.1 us
    dot_general x1, matrix products, per_device(): jnp.einsum('ocpn,ocnq->ocpq', arrived, chosen, preferred_element_type=jnp...  32.5 us
    add x1, local copies, waits for them, and re-layouts, per_device(): fock_part + jnp.einsum('Psce,Psped->Pspcd', left_fock, shaped, preferred_...  31.1 us
    dot_general x1, matrix products, per_device(): jnp.einsum('Psce,Psped->Pspcd', left_fock, shaped, preferred_element_type...  28.8 us
    reshape x1, local copies, waits for them, and re-layouts, per_device(): fock_part.reshape(local_tiles, slot_count, pair_rows, tile_size)  27.9 us
    reshape x1, local copies, waits for them, and re-layouts, per_device(): amplitudes.reshape(local_tiles, slot_count, pair_rows, tile_width, tile_w...  24.1 us
    dot_general x1, matrix products, per_device(): jnp.einsum('Pspce,Psed->Pspcd', shaped, right_fock, preferred_element_typ...  24.1 us
  transfers between devices with their start and end apart: 4, of which 1 were waited for; matrix products, arithmetic and copies ran while one was open for 37% of the time, Pallas kernels for 0%

commit v1 on v0

v1 whole, which is shorter than its diff:
```python
import functools

import jax
import jax.numpy as jnp
from jax import lax
from jax.experimental import pallas as pl
from jax.experimental.pallas import tpu as pltpu
from jax.sharding import PartitionSpec as P

AXES = ("occ", "vir")
CHUNKS = 4
EXTRA = 2
VMEM_LIMIT = 48 * 1024 * 1024


def pack_kernel(owner_ref, count_ref, amp_ref, *refs):
    outs, (slot_ref, sem) = refs[:-2], refs[-2:]
    devices, rows, width = outs[0].shape
    owners = slot_ref.shape[0]
    parts = devices // owners
    tiles, slots = owner_ref.shape
    for o in range(owners):
        slot_ref[o] = 0
    for t in reversed(range(tiles)):
        for s in range(slots):

            @pl.when(s < count_ref[t])
            def _():
                slot_ref[owner_ref[t, s]] = t * slots + s

    def copies(o):
        entry = slot_ref[o]
        t, s = entry // slots, entry % slots
        for v in range(parts):
            for i, out in enumerate(outs):
                first = (v * len(outs) + i) * width
                yield pltpu.make_async_copy(
                    amp_ref.at[t, s, :, pl.ds(first, width)], out.at[o * parts + v], sem
                )

    def start(o, carry):
        for copy in copies(o):
            copy.start()
        return carry

    def wait(o, carry):
        for copy in copies(o):
            copy.wait()
        return carry

    lax.fori_loop(0, owners, start, 0)
    lax.fori_loop(0, owners, wait, 0)


def pack(tile_owner, tile_counts, amplitudes, owners, parts):
    _, _, rows, size = amplitudes.shape
    width = size // parts // CHUNKS
    return pl.pallas_call(
        pack_kernel,
        grid_spec=pltpu.PrefetchScalarGridSpec(
            num_scalar_prefetch=2,
            grid=(1,),
            in_specs=[pl.BlockSpec(memory_space=pl.ANY)],
            out_specs=[pl.BlockSpec(memory_space=pl.ANY)] * CHUNKS,
            scratch_shapes=[pltpu.SMEM((owners,), jnp.int32), pltpu.SemaphoreType.DMA],
        ),
        out_shape=[jax.ShapeDtypeStruct((owners * parts, rows, width), amplitudes.dtype)] * CHUNKS,
        name="pack_first",
    )(tile_owner, tile_counts, amplitudes)


def pack_extra_kernel(pick_ref, amp_ref, out_ref, sem):
    parts, extra, _, width = out_ref.shape
    copies = [
        pltpu.make_async_copy(
            amp_ref.at[1, pick_ref[j], :, pl.ds(v * width, width)], out_ref.at[v, j], sem
        )
        for j in range(extra)
        for v in range(parts)
    ]
    for copy in copies:
        copy.start()
    for copy in copies:
        copy.wait()


def pack_extra(pick, amplitudes, parts):
    _, _, rows, size = amplitudes.shape
    return pl.pallas_call(
        pack_extra_kernel,
        grid_spec=pltpu.PrefetchScalarGridSpec(
            num_scalar_prefetch=1,
            grid=(1,),
            in_specs=[pl.BlockSpec(memory_space=pl.ANY)],
            out_specs=pl.BlockSpec(memory_space=pl.ANY),
            scratch_shapes=[pltpu.SemaphoreType.DMA],
        ),
        out_shape=jax.ShapeDtypeStruct((parts, EXTRA, rows, size // parts), amplitudes.dtype),
        name="pack_extra",
    )(pick, amplitudes)


def ladder_kernel(block_ref, tile_ref, row_ref, count_ref, acc_in_ref, x_ref, panel_ref, acc_ref):
    i = pl.program_id(0)

    @pl.when(i == 0)
    def _():
        acc_ref[...] = acc_in_ref[...]

    @pl.when(i < count_ref[0])
    def _():
        row = row_ref[i]
        acc_ref[row] = acc_ref[row] + jnp.dot(
            x_ref[0], panel_ref[0], preferred_element_type=jnp.float32
        )


def ladder(lists, acc, blocks, panels, chunk):
    block, tile, row, count = lists
    steps = block.shape[0]
    _, rows, width = blocks.shape
    panel_width = panels.shape[2]
    whole = pl.BlockSpec(acc.shape, lambda i, *_: (0, 0, 0))
    return pl.pallas_call(
        ladder_kernel,
        grid_spec=pltpu.PrefetchScalarGridSpec(
            num_scalar_prefetch=4,
            grid=(steps,),
            in_specs=[
                whole,
                pl.BlockSpec((1, rows, width), lambda i, b, t, r, c: (b[i], 0, 0)),
                pl.BlockSpec((1, width, panel_width), lambda i, b, t, r, c: (t[i], chunk, 0)),
            ],
            out_specs=whole,
        ),
        out_shape=jax.ShapeDtypeStruct(acc.shape, jnp.float32),
        input_output_aliases={4: 0},
        compiler_params=pltpu.CompilerParams(vmem_limit_bytes=VMEM_LIMIT),
        cost_estimate=pl.CostEstimate(
            flops=2 * steps * rows * width * panel_width,
            bytes_accessed=2 * steps * width * (rows + panel_width),
            transcendentals=0,
        ),
        name="ladder",
    )(block, tile, row, count, acc, blocks, panels)


def residual_kernel(
    owner_ref,
    local_ref,
    count_ref,
    map_ref,
    amp_ref,
    weight_ref,
    left_ref,
    right_ref,
    out_ref,
    diag_ref,
    rows_ref,
    turned_ref,
):
    slots = owner_ref.shape[1]
    i = pl.program_id(0)
    used = i % slots < count_ref[i // slots]
    _, _, rows, size = amp_ref.shape
    vt = left_ref.shape[1]
    half = vt // 2
    lanes = 2 * vt
    pieces = size // lanes
    wide = diag_ref.shape[0]

    @pl.when(i == 0)
    def _():
        diag_ref[...] = jnp.zeros_like(diag_ref)

    @pl.when(jnp.logical_not(used))
    def _():
        out_ref[...] = jnp.zeros_like(out_ref)

    @pl.when(used)
    def _():
        for k in range(wide // vt):
            diag_ref[k * vt : (k + 1) * vt, k * vt : (k + 1) * vt] = right_ref[0]
        low = lax.broadcasted_iota(jnp.int32, (half, lanes), 1) < vt
        for k in range(pieces):
            rows_ref[pl.ds(k, rows, stride=pieces), :] = amp_ref[
                0, 0, :, k * lanes : (k + 1) * lanes
            ].astype(jnp.float32)
        for j in range(rows // 2):
            even = rows_ref[(2 * j) * pieces : (2 * j + 1) * pieces, :]
            odd = rows_ref[(2 * j + 1) * pieces : (2 * j + 2) * pieces, :]
            top = jnp.where(low, even, pltpu.roll(odd, vt, 1))
            bottom = jnp.where(low, pltpu.roll(even, vt, 1), odd)
            turned_ref[:, j * lanes : (j + 1) * lanes] = jnp.concatenate([top, bottom], 0).astype(
                jnp.bfloat16
            )
        for j in range(rows // 2):
            both = jnp.dot(
                left_ref[0],
                turned_ref[:, j * lanes : (j + 1) * lanes],
                preferred_element_type=jnp.float32,
            )
            top, bottom = both[:half], both[half:]
            rows_ref[(2 * j) * pieces : (2 * j + 1) * pieces, :] = jnp.where(
                low, top, pltpu.roll(bottom, vt, 1)
            )
            rows_ref[(2 * j + 1) * pieces : (2 * j + 2) * pieces, :] = jnp.where(
                low, pltpu.roll(top, vt, 1), bottom
            )
        for j in range(size // wide):
            at = slice(j * wide, (j + 1) * wide)
            block = amp_ref[0, 0, :, at]
            total = jnp.dot(weight_ref[0], block, preferred_element_type=jnp.float32)
            total = total + jnp.dot(block, diag_ref[...], preferred_element_type=jnp.float32)
            for k in range(wide // lanes):
                piece = j * (wide // lanes) + k
                left = rows_ref[pl.ds(piece, rows, stride=pieces), :]
                out_ref[0, 0, :, piece * lanes : (piece + 1) * lanes] = (
                    total[:, k * lanes : (k + 1) * lanes] + left
                ).astype(jnp.bfloat16)


def residual(tile_owner, tile_local, tile_counts, pair_map, amplitudes, hole_weight, fock_tiles, per_owner):
    tiles, slots, rows, size = amplitudes.shape
    tile_count, vt, _ = fock_tiles.shape
    left = fock_tiles.reshape(tile_count, vt // 2, 2, vt // 2, 2).transpose(0, 2, 1, 4, 3)
    left = left.reshape(tile_count, vt, vt)
    wide = 4 * vt

    def ident(i, owner, local, pairs):
        t, s = i // slots, i % slots
        return pairs[owner[t, s] * per_owner + local[t, s]]

    return pl.pallas_call(
        residual_kernel,
        grid_spec=pltpu.PrefetchScalarGridSpec(
            num_scalar_prefetch=4,
            grid=(tiles * slots,),
            in_specs=[
                pl.BlockSpec((1, 1, rows, size), lambda i, *_: (i // slots, i % slots, 0, 0)),
                pl.BlockSpec((1, rows, rows), lambda i, *_: (i // slots, 0, 0)),
                pl.BlockSpec(
                    (1, vt, vt), lambda i, o, l, c, m: (ident(i, o, l, m) // tile_count, 0, 0)
                ),
                pl.BlockSpec(
                    (1, vt, vt), lambda i, o, l, c, m: (ident(i, o, l, m) % tile_count, 0, 0)
                ),
            ],
            out_specs=pl.BlockSpec((1, 1, rows, size), lambda i, *_: (i // slots, i % slots, 0, 0)),
            scratch_shapes=[
                pltpu.VMEM((wide, wide), jnp.bfloat16),
                pltpu.VMEM((rows * size // (2 * vt), 2 * vt), jnp.float32),
                pltpu.VMEM((vt, rows * vt), jnp.bfloat16),
            ],
        ),
        out_shape=jax.ShapeDtypeStruct(amplitudes.shape, jnp.bfloat16),
        compiler_params=pltpu.CompilerParams(vmem_limit_bytes=VMEM_LIMIT),
        cost_estimate=pl.CostEstimate(
            flops=40 * amplitudes.size * vt, bytes_accessed=4 * amplitudes.size, transcendentals=0
        ),
        name="residual",
    )(tile_owner, tile_local, tile_counts, pair_map, amplitudes, hole_weight, left, fock_tiles)


def squeeze_list(valid, *columns):
    length = valid.shape[0]
    at = jnp.arange(length, dtype=jnp.int32)
    ahead = jnp.cumsum(valid.astype(jnp.int32))
    count = ahead[-1]
    wanted = jnp.minimum(at, jnp.maximum(count - 1, 0))
    chosen = (valid[None, :] & (ahead[None, :] - 1 == wanted[:, None])).astype(jnp.int32)
    return [jnp.sum(chosen * c[None, :], axis=1) for c in columns] + [count.reshape(1)]


def per_device(
    amplitudes,
    tile_counts,
    tile_owner,
    tile_local,
    pair_map,
    hole_weight,
    fock_tiles,
    ladder_panels,
):
    owners, parts = lax.axis_size("occ"), lax.axis_size("vir")
    per_owner, part_rows, panel_width = ladder_panels.shape
    tiles, slots, pair_rows, tile_size = amplitudes.shape
    devices = owners * parts
    slot_at = jnp.arange(slots, dtype=jnp.int32)

    sent = pack(tile_owner, tile_counts, amplitudes, owners, parts)

    mine = jnp.concatenate([tile_owner, tile_local, tile_counts[:, None]], axis=1)
    table = lax.all_gather(mine, AXES, axis=0, tiled=True).reshape(devices, tiles, 2 * slots + 1)
    owner, local = table[:, :, :slots], table[:, :, slots : 2 * slots]
    used = slot_at < table[:, :, 2 * slots :]
    repeat = used[:, 1] & jnp.any(
        used[:, 0, :, None] & (owner[:, 0, :, None] == owner[:, 1, None, :]), axis=1
    )
    turn = jnp.cumsum(repeat.astype(jnp.int32), axis=1) - repeat
    rounds = (jnp.max(jnp.sum(repeat, axis=1)) + EXTRA - 1) // EXTRA
    hit = used & (owner == lax.axis_index("occ"))
    named = jnp.any(hit, axis=2)
    tile = jnp.sum(jnp.where(hit, local, 0), axis=2)
    device = jnp.arange(devices, dtype=jnp.int32)
    first = squeeze_list(
        named[:, 0] | named[:, 1],
        device,
        jnp.where(named[:, 0], tile[:, 0], tile[:, 1]),
        jnp.where(named[:, 0], 2 * device, 2 * device + 1),
    )
    doubled = named[:, 0] & named[:, 1]
    my_turn = jnp.sum(jnp.where(hit[:, 1], turn, 0), axis=1)

    my_used = slot_at < tile_counts[:, None]
    my_repeat = my_used[1] & jnp.any(
        my_used[0, :, None] & (tile_owner[0, :, None] == tile_owner[1, None, :]), axis=0
    )
    own_turn = jnp.cumsum(my_repeat.astype(jnp.int32)) - my_repeat

    def extra_blocks(k):
        wanted = k * EXTRA + jnp.arange(EXTRA, dtype=jnp.int32)
        pick = jnp.sum(
            jnp.where(my_repeat & (own_turn == wanted[:, None]), slot_at, 0), axis=1
        ).astype(jnp.int32)
        packed = pack_extra(pick, amplitudes, parts)
        swapped = lax.all_to_all(packed, "vir", split_axis=0, concat_axis=0, tiled=True)
        got = lax.all_gather(swapped, "occ", axis=0, tiled=True)
        return got.reshape(devices * EXTRA, pair_rows, part_rows)

    def extra_list(k):
        return squeeze_list(
            doubled & (my_turn // EXTRA == k),
            device * EXTRA + my_turn % EXTRA,
            tile[:, 1],
            2 * device + 1,
        )

    second = extra_blocks(0)
    arrived = [lax.all_to_all(x, AXES, split_axis=0, concat_axis=0, tiled=True) for x in sent]
    local_residual = residual(
        tile_owner, tile_local, tile_counts, pair_map, amplitudes, hole_weight, fock_tiles, per_owner
    )
    acc = jnp.zeros((devices * tiles, pair_rows, panel_width), jnp.float32)
    acc = ladder(extra_list(0), acc, second, ladder_panels, 0)
    for chunk, blocks in enumerate(arrived):
        acc = ladder(first, acc, blocks, ladder_panels, chunk)

    def more(k, acc):
        return ladder(extra_list(k), acc, extra_blocks(k), ladder_panels, 0)

    acc = lax.fori_loop(1, rounds, more, acc)
    ladder_panel = lax.psum_scatter(acc, AXES, scatter_dimension=0, tiled=True)
    return (local_residual, ladder_panel.astype(jnp.bfloat16))


def solution(mesh):
    in_specs = (
        P(("occ", "vir"), None, None, None),
        P(("occ", "vir")),
        P(("occ", "vir"), None),
        P(("occ", "vir"), None),
        P(),
        P(("occ", "vir"), None, None),
        P(),
        P("occ", "vir", None),
    )
    out_specs = (P(("occ", "vir"), None, None, None), P(("occ", "vir"), None, None))
    return jax.shard_map(
        per_device, mesh=mesh, in_specs=in_specs, out_specs=out_specs, check_vma=False
    )
```

time: 592 us -> 761 us (1.29)
  Pallas kernels: 0 us -> 355 us
  blocking collectives: 0 us -> 185 us
  matrix products: 123 us -> 0 us
  local copies, waits for them, and re-layouts: 124 us -> 6.63 us
  starting transfers between devices: 87.4 us -> 7.84 us
  waiting for transfers between devices: 232 us -> 190 us
    pallas_call x0 -> x8, Pallas kernels: none -> 355 us  [the longest x1 256 us: pack(): pl.pallas_call(pack_kernel, grid_spec=pltpu.PrefetchScalarGridSpec(num_sc...]
    all_to_all x3 -> x2, waiting for transfers between devices: 232 us -> 48.8 us  [per_device(): lax.all_to_all(x, AXES, split_axis=0, concat_axis=0, tiled=True)]
    reduce_scatter x0 -> x1, waiting for transfers between devices: none -> 140 us  [per_device(): ladder_panel = lax.psum_scatter(acc, AXES, scatter_dimension=0, tiled=True)]
    dot_general x7 -> x0, matrix products: 123 us -> none  [the longest x1 32.5 us: per_device(): jnp.einsum('ocpn,ocnq->ocpq', arrived, chosen, preferred_element_type=jnp...]
    all_to_all x0 -> x3, blocking collectives: none -> 115 us  [the longest x2 108 us: per_device(): lax.all_to_all(x, AXES, split_axis=0, concat_axis=0, tiled=True)]
    all_to_all x3 -> x2, starting transfers between devices: 87.4 us -> 7.8 us  [per_device(): lax.all_to_all(x, AXES, split_axis=0, concat_axis=0, tiled=True)]
    all_gather x0 -> x1, blocking collectives: none -> 69.5 us  [per_device(): lax.all_gather(mine, AXES, axis=0, tiled=True)]
    reshape x3 -> x1, local copies, waits for them, and re-layouts: 52.1 us -> 0.25 us  [residual(): left = left.reshape(tile_count, vt, vt)]
  transfers between devices with their start and end apart: 4 -> 4, of which waited for: 1 -> 2; matrix products, arithmetic and copies ran while one was open for 37% -> 1% of each run, Pallas kernels for 0% -> 40%
where the time goes in v1:
time: 761 us; the launch traced here: 764 us
  Pallas kernels  355 us (47%)
  waiting for transfers between devices  190 us (25%)
  blocking collectives  185 us (24%)
  between operations  16.4 us (2%)
  starting transfers between devices  7.84 us (1%)
    pallas_call x1, Pallas kernels, pack(): pl.pallas_call(pack_kernel, grid_spec=pltpu.PrefetchScalarGridSpec(num_sc...  256 us
    reduce_scatter x1, waiting for transfers between devices, per_device(): ladder_panel = lax.psum_scatter(acc, AXES, scatter_dimension=0, tiled=True)  140 us
    all_to_all x2, blocking collectives, per_device(): lax.all_to_all(x, AXES, split_axis=0, concat_axis=0, tiled=True)  108 us
    all_gather x1, blocking collectives, per_device(): lax.all_gather(mine, AXES, axis=0, tiled=True)  69.5 us
    all_to_all x2, waiting for transfers between devices, per_device(): lax.all_to_all(x, AXES, split_axis=0, concat_axis=0, tiled=True)  48.8 us
    pallas_call x5, Pallas kernels, ladder(): pl.pallas_call(ladder_kernel, grid_spec=pltpu.PrefetchScalarGridSpec(num_...  40.3 us
    pallas_call x1, Pallas kernels, pack_extra(): pl.pallas_call(pack_extra_kernel, grid_spec=pltpu.PrefetchScalarGridSpec(...  33.5 us
    pallas_call x1, Pallas kernels, residual(): pl.pallas_call(residual_kernel, grid_spec=pltpu.PrefetchScalarGridSpec(nu...  24.8 us
  transfers between devices with their start and end apart: 4, of which 2 were waited for; matrix products, arithmetic and copies ran while one was open for 1% of the time, Pallas kernels for 40%

profile of v1, /device:TPU:0, one launch (start us, length us, event | category | flops | bytes accessed | tf_op | source)
XLA Modules:
  0.0 764.5 jit_solution(14099687037445454367)
XLA Ops:
  7.2 0.7 iota_compare_fusion.1
  7.9 0.8 slice_bitcast_fusion.6
  9.0 0.6 fusion.23.pick_ref
  9.6 33.5 %pack_extra.7 = bf16[2,2,64,2048]{3,2,1,0:T(8,128)(2,1)} custom-call(s32[2]{0:T(128)} %fusion.23.pick_ref, bf16[2,8,64,4096]{3,2,1,0:T(8,128)(2,1)} %amp_ref.5), custom_call_target="tpu_custom_call" | custom-call | tf_op jit(solution)/shard_map/pack_extra/pallas_call | solution.py:89
  43.2 6.6 all_to_all.38
  49.8 255.9 %pack_first.1 = (bf16[32,64,512]{2,1,0:T(8,128)(2,1)}, bf16[32,64,512]{2,1,0:T(8,128)(2,1)}, bf16[32,64,512]{2,1,0:T(8,128)(2,1)}, bf16[32,64,512]{2,1,0:T(8,128)(2,1)}) custom-call(s32[2,8]{1,0:T(2,128)} %owner_ref.3, s32[2]{0:T(128)} %count_ref.3, bf16[2,8,64,4096]{3,2,1,0:T(8,128)(2,1)} %amp_ref.5), custom_call_target="tpu_custom_call" | custom-call | tf_op jit(solution)/shard_map/pack_first/pallas_call | solution.py:58
  305.8 56.1 %all_to_all.39.x_ref = bf16[32,64,512]{2,1,0:T(8,128)(2,1)} all-to-all(bf16[32,64,512]{2,1,0:T(8,128)(2,1)} %get-tuple-element.303), channel_id=1, replica_groups=mesh['occ'=16,'vir'=2] {'occ','vir'}, dimensions={0} | all-to-all | bytes 4194304 | tf_op jit(solution)/shard_map/all_to_all | solution.py:340
  361.9 52.3 %all_to_all.40.x_ref = bf16[32,64,512]{2,1,0:T(8,128)(2,1)} all-to-all(bf16[32,64,512]{2,1,0:T(8,128)(2,1)S(1)} %copy-done.11), channel_id=1, replica_groups=mesh['occ'=16,'vir'=2] {'occ','vir'}, dimensions={0} | all-to-all | bytes 4194304 | tf_op jit(solution)/shard_map/all_to_all | solution.py:340
  414.2 3.7 all-to-all-start.4
  418.0 48.8 %all-to-all-done.4.x_ref = bf16[32,64,512]{2,1,0:T(8,128)(2,1)S(1)} async-done(((bf16[32,64,512]{2,1,0:T(8,128)(2,1)}), bf16[32,64,512]{2,1,0:T(8,128)(2,1)S(1)}, u32[]{:S(2)}, u32[]{:S(2)}) %all-to-all-start.4) | async-done | bytes 2097184 | tf_op jit(solution)/shard_map/all_to_all | solution.py:340
  466.8 4.1 all-to-all-start.5
  471.0 69.5 %all-gather = s32[32,2,17]{2,1,0:T(2,128)S(1)} all-gather(s32[1,2,17]{2,1,0:T(2,128)S(1)} %add_bitcast_fusion), channel_id=1, replica_groups=mesh['occ'=16,'vir'=2] {'occ','vir'}, dimensions={0}, use_global_device_ids=true | all-gather | bytes 4488 | tf_op jit(solution)/shard_map/all_gather | solution.py:294
  541.3 0.6 reduce_max.9
  546.6 4.9 ladder.11.acc_in_ref
  551.5 1.4 copy-done.8
  552.9 7.5 ladder.12.acc_in_ref
  560.4 7.3 ladder.13.acc_in_ref
  567.7 7.3 ladder.14.acc_in_ref
  575.1 13.2 %ladder.15 = f32[64,64,128]{2,1,0:T(8,128)} custom-call(s32[32]{0:T(128)S(1)} %get-tuple-element.451.block_ref, s32[32]{0:T(128)S(1)} %get-tuple-element.450.tile_ref, s32[32]{0:T(128)S(1)} %get-tuple-element.449.row_ref, s32[1]{0:T(128)} %bitcast.6.count_ref, f32[64,64,128]{2,1,0:T(8,128)} %ladder.14.acc_in_ref, ...), custom_call_target="tpu_custom_call", output_to_operand_aliasing={{}: (4, {})} | custom-call | flops 268435456 | bytes 6291456 | tf_op jit(solution)/shard_map/ladder/pallas_call | solution.py:124
  588.3 0.7 reduce-scatter.2.cloned.1.call-update
  589.8 1.1 copy.111
  591.2 24.8 %residual.1 = bf16[2,8,64,4096]{3,2,1,0:T(8,128)(2,1)} custom-call(s32[2,8]{1,0:T(2,128)S(1)} %copy-done.3, s32[2,8]{1,0:T(2,128)S(1)} %copy-done.4, s32[2]{0:T(128)S(1)} %copy-done.5, s32[256]{0:T(256)S(1)} %copy-done.7, bf16[2,8,64,4096]{3,2,1,0:T(8,128)(2,1)} %get-tuple-element.681, bf16[2,64,64]{2,1,0:T(8,128)(2,1)S(1)} %copy-done.6, ...), custom_call_target="tpu_custom_call" | custom-call | flops 10737418240 | bytes 16777216 | tf_op jit(solution)/shard_map/residual/pallas_call | solution.py:234
  616.0 140.2 %reduce-scatter.2.cloned.1.call-done = f32[2,64,128]{2,1,0:T(8,128)} async-done(((f32[64,64,128]{2,1,0:T(8,128)}), f32[2,64,128]{2,1,0:T(8,128)}) %reduce-scatter.2.cloned.1.call-update) | async-done | bytes 65552 | tf_op jit(solution)/shard_map/reduce_scatter | solution.py:353
  756.2 1.5 convert_element_type.56
  (77 shorter events, 4.8 us)
Async XLA Ops:
  7.2 539.1 %all-gather.4.cloned.1.call-start = ((), (), s32[]{:S(2)}) async-start(), calls=%async_computation.7 | async-start | bytes 17825792 | tf_op jit(solution)/shard_map/all_gather | solution.py:328
  305.8 56.1 %copy-start.11 = (bf16[32,64,512]{2,1,0:T(8,128)(2,1)S(1)}, bf16[32,64,512]{2,1,0:T(8,128)(2,1)}, u32[]{:S(2)}) copy-start(bf16[32,64,512]{2,1,0:T(8,128)(2,1)} %get-tuple-element.304) | copy-start | bytes 6291460
  414.2 3.7 copy-start.5
  414.2 52.6 %all-to-all-start.4 = ((bf16[32,64,512]{2,1,0:T(8,128)(2,1)}), bf16[32,64,512]{2,1,0:T(8,128)(2,1)S(1)}, u32[]{:S(2)}, u32[]{:S(2)}) async-start(bf16[32,64,512]{2,1,0:T(8,128)(2,1)} %get-tuple-element.305), calls=%async_computation.4 | async-start | bytes 4194304 | tf_op jit(solution)/shard_map/all_to_all | solution.py:340
  466.8 4.2 copy-start.3
  466.8 4.2 copy-start.4
  466.8 108.3 %all-to-all-start.5 = ((bf16[32,64,512]{2,1,0:T(8,128)(2,1)}), bf16[32,64,512]{2,1,0:T(8,128)(2,1)}, u32[]{:S(2)}, u32[]{:S(2)}) async-start(bf16[32,64,512]{2,1,0:T(8,128)(2,1)} %get-tuple-element.306), calls=%async_computation.5 | async-start | bytes 4194304 | tf_op jit(solution)/shard_map/all_to_all | solution.py:340
  546.3 6.6 slice-start
  546.6 6.3 copy-start.1
  546.6 6.3 slice-start.1
  551.5 1.4 copy-start.8
  552.9 7.5 copy-start
  588.3 0.9 copy-start.2
  588.3 167.9 %reduce-scatter.2.cloned.1.call-start = ((), (), s32[]{:S(2)}) async-start(), calls=%async_computation.8 | async-start | bytes 2162688 | tf_op jit(solution)/shard_map/reduce_scatter | solution.py:353
  589.2 1.9 copy-start.6
  589.2 1.9 copy-start.7
Sparse Core Ops, SparseCore 0:
  50.0 194.3 all-gather.3
  591.4 164.7 reduce-scatter.1
